TPU v7x, 32 devices: a whole 2x2x4 slice. The times are simulated.
32 devices in a mesh: dp: 8 (over y, x, core), fsdp: 4 (over z).
Axes of the slice: x: 2, y: 2, z: 4, core: 2. Of those that a mesh axis runs over, the one named last changes fastest.
Arguments:
- rollout_rows: bfloat16 [4096, 8192], P(('dp', 'fsdp')), may hold values from -6 to 6
- lengths: int32 [32, 8], P(('dp', 'fsdp')), may hold values from 1 to 32, as said below
- dest: int32 [32, 8], P(('dp', 'fsdp')), may hold values from 0 to 7, as said below
- offset: int32 [32, 8], P(('dp', 'fsdp')), may hold values from 0 to 96, as said below
- query: bfloat16 [4096, 4096], P(('dp', 'fsdp')), may hold values from -100 to 100
- key_rows: bfloat16 [4096, 512], P(('dp', 'fsdp')), may hold values from -5 to 5
- value_weight: bfloat16 [8192, 512], P('fsdp'), may hold values from -0.0625 to 0.0625
- d_out: bfloat16 [4096, 4096], P(('dp', 'fsdp')), may hold values from -6 to 6
Outputs:
- attn_out: bfloat16 [4096, 4096], P(('dp', 'fsdp'))
- grad_query: bfloat16 [4096, 4096], P(('dp', 'fsdp'))
- grad_key: bfloat16 [4096, 512], P(('dp', 'fsdp'))
- grad_input: bfloat16 [4096, 8192], P(('dp', 'fsdp'))
- grad_weight: float32 [8192, 512], P(('dp', 'fsdp'))
Inputs may be any that keep to these rules, and one draw needn't show every extreme that they name: Each rollout device's 8 lengths sum to 128. `dest`: the learner has the sender's fsdp index; the sequences of one device go to 8 different learner devices. `offset`: the sequences that a learner device receives cover its 128 rows exactly once; on every learner device the last of them is one of 32 rows.
All inputs are finite; a program needn't handle non-finite values.
Results may differ from a plain program's by a relative error of at most 0.006.
Values may be sent and summed in bfloat16 or wider, within the bound.
A program may use at most 128 MiB of HBM per device.

v0:
```python
import math
import jax
import jax.numpy as jnp
from jax import lax
from jax.sharding import PartitionSpec as P

HEAD_SIZE = 128
QUERY_HEADS = 32
KEY_VALUE_HEADS = 4


def attend(block_queries, block_keys, block_values, segment, gradient_block):
    row_count_total = block_queries.shape[0]
    share_ratio = QUERY_HEADS // KEY_VALUE_HEADS
    score_scale = 1.0 / math.sqrt(HEAD_SIZE)
    heads_queries = block_queries.reshape(row_count_total, KEY_VALUE_HEADS, share_ratio, HEAD_SIZE)
    heads_keys = block_keys.reshape(row_count_total, KEY_VALUE_HEADS, HEAD_SIZE)
    heads_values = block_values.reshape(row_count_total, KEY_VALUE_HEADS, HEAD_SIZE)
    gradient_heads = gradient_block.reshape(
        row_count_total, KEY_VALUE_HEADS, share_ratio, HEAD_SIZE
    )
    logit_scores = (
        jnp.einsum("euaz,nuz->uaen", heads_queries, heads_keys, preferred_element_type=jnp.float32)
        * score_scale
    )
    position = jnp.arange(row_count_total, dtype=jnp.int32)
    allowed = (segment[:, None] == segment[None, :]) & (position[None, :] <= position[:, None])
    logit_scores = jnp.where(allowed, logit_scores, -1e30)
    highest = jnp.max(logit_scores, axis=-1, keepdims=True)
    expo = jnp.exp(logit_scores - highest)
    probs = expo / jnp.sum(expo, axis=-1, keepdims=True)
    probs_reduced = probs.astype(jnp.bfloat16)
    attention_output = jnp.einsum(
        "yxmd,dya->myxa", probs_reduced, heads_values, preferred_element_type=jnp.float32
    )
    attention_output = attention_output.reshape(row_count_total, QUERY_HEADS * HEAD_SIZE).astype(
        jnp.bfloat16
    )
    gradient_probs = jnp.einsum(
        "euaz,nuz->uaen", gradient_heads, heads_values, preferred_element_type=jnp.float32
    )
    value_gradient = jnp.einsum(
        "lbjm,jlbw->mlw", probs_reduced, gradient_heads, preferred_element_type=jnp.float32
    )
    value_gradient = value_gradient.reshape(row_count_total, KEY_VALUE_HEADS * HEAD_SIZE).astype(
        jnp.bfloat16
    )
    inner = jnp.sum(probs * gradient_probs, axis=-1, keepdims=True)
    gradient_scores = (probs * (gradient_probs - inner) * score_scale).astype(jnp.bfloat16)
    query_gradient = jnp.einsum(
        "yxmd,dya->myxa", gradient_scores, heads_keys, preferred_element_type=jnp.float32
    )
    key_gradient = jnp.einsum(
        "lbjm,jlbw->mlw", gradient_scores, heads_queries, preferred_element_type=jnp.float32
    )
    return (
        attention_output,
        query_gradient.reshape(row_count_total, QUERY_HEADS * HEAD_SIZE).astype(jnp.bfloat16),
        key_gradient.reshape(row_count_total, KEY_VALUE_HEADS * HEAD_SIZE).astype(jnp.bfloat16),
        value_gradient,
    )


def tables(plan, tok_rows):
    seq_len, dest, offset = (plan[:, 0], plan[:, 1], plan[:, 2])
    order = jnp.arange(seq_len.shape[1], dtype=jnp.int32)
    earlier = order[None, :] < order[:, None]
    starts = jnp.sum(jnp.where(earlier[None], seq_len[:, None, :], 0), axis=2)
    rows = jnp.arange(tok_rows, dtype=jnp.int32)[None, :, None]
    inside = (rows >= starts[:, None, :]) & (rows < (starts + seq_len)[:, None, :])
    landing = (dest * tok_rows + offset - starts)[:, None, :] + rows
    return jnp.sum(jnp.where(inside, landing, 0), axis=2).reshape(-1)


def senders(plan, me, tok_rows):
    seq_len, dest, offset = (plan[:, 0], plan[:, 1], plan[:, 2])
    mine = dest == me
    land_off = jnp.sum(jnp.where(mine, offset, 0), axis=1)
    land_len = jnp.sum(jnp.where(mine, seq_len, 0), axis=1)
    rows = jnp.arange(tok_rows, dtype=jnp.int32)[:, None]
    inside = (rows >= land_off[None, :]) & (rows < (land_off + land_len)[None, :])
    source = jnp.arange(plan.shape[0], dtype=jnp.int32)
    return jnp.sum(jnp.where(inside, source[None, :], 0), axis=1)


def local(rollout_rows, lengths, dest, offset, query, key_rows, value_weight, d_out):
    n_dp = lax.axis_size("dp")
    n_fsdp = lax.axis_size("fsdp")
    me = lax.axis_index("dp")
    tok_rows = rollout_rows.shape[0]
    column = tok_rows * n_dp
    plan = lax.all_gather(jnp.concatenate([lengths, dest, offset], axis=0), "dp", axis=0)
    shared = lax.all_to_all(rollout_rows, "dp", split_axis=1, concat_axis=0, tiled=True)
    block = value_weight.shape[0] // n_dp
    piece = lax.dynamic_slice_in_dim(value_weight, me * block, block, axis=0)
    pairs = [(a * n_fsdp + b, b * n_dp + a) for a in range(n_dp) for b in range(n_fsdp)]
    piece = lax.ppermute(piece, ("dp", "fsdp"), pairs)
    weight = lax.all_gather(piece, "fsdp", axis=0, tiled=True)
    landing = tables(plan, tok_rows)
    pick = (jnp.arange(column, dtype=jnp.int32)[:, None] == landing[None, :]).astype(jnp.bfloat16)
    rows = jnp.dot(pick, shared, preferred_element_type=jnp.float32).astype(jnp.bfloat16)
    partial = jnp.dot(rows, weight, preferred_element_type=jnp.float32).astype(jnp.bfloat16)
    parts = lax.all_to_all(
        partial.reshape(n_dp, tok_rows, partial.shape[1]),
        "dp",
        split_axis=0,
        concat_axis=0,
        tiled=True,
    )
    values = jnp.sum(parts.astype(jnp.float32), axis=0).astype(jnp.bfloat16)
    attention_output, query_gradient, key_gradient, value_gradient = attend(
        query, key_rows, values, senders(plan, me, tok_rows), d_out
    )
    gathered = lax.all_gather(value_gradient, "dp", axis=0, tiled=True)
    grad_weight = lax.psum_scatter(
        lax.dot_general(
            rows, gathered, (((0,), (0,)), ((), ())), preferred_element_type=jnp.float32
        ),
        "fsdp",
        scatter_dimension=0,
        tiled=True,
    )
    grad_weight = grad_weight * (1.0 / math.sqrt(column * n_fsdp))
    share = lax.dot_general(
        gathered, weight, (((1,), (1,)), ((), ())), preferred_element_type=jnp.float32
    ).astype(jnp.bfloat16)
    grad_input = lax.all_to_all(share, "dp", split_axis=0, concat_axis=1, tiled=True)
    return (attention_output, query_gradient, key_gradient, grad_input, grad_weight)


def solution(mesh):
    in_specs = (
        P(("dp", "fsdp"), None),
        P(("dp", "fsdp"), None),
        P(("dp", "fsdp"), None),
        P(("dp", "fsdp"), None),
        P(("dp", "fsdp"), None),
        P(("dp", "fsdp"), None),
        P("fsdp", None),
        P(("dp", "fsdp"), None),
    )
    out_specs = (
        P(("dp", "fsdp"), None),
        P(("dp", "fsdp"), None),
        P(("dp", "fsdp"), None),
        P(("dp", "fsdp"), None),
        P(("dp", "fsdp"), None),
    )
    return jax.shard_map(local, mesh=mesh, in_specs=in_specs, out_specs=out_specs, check_vma=False)
```

profile of v0, /device:TPU:0, one launch (start us, length us, event | category | flops | bytes accessed | tf_op | source)
XLA Modules:
  0.0 167.1 jit_solution(17855206566767428514)
XLA Ops:
  7.2 0.0 copy-start
  7.2 0.0 all-gather.7.cloned.1.call-start
  7.2 0.8 add_bitcast_fusion
  8.1 10.3 %all-gather.1 = s32[8,3,8]{2,1,0:T(4,128)S(1)} all-gather(s32[1,3,8]{2,1,0:T(4,128)S(1)} %add_bitcast_fusion), channel_id=2, replica_groups=mesh['dp'=8,'fsdp'=4] {'dp'}, dimensions={0}, use_global_device_ids=true | all-gather | bytes 864 | tf_op jit(solution)/shard_map/all_gather | solution.py:92
  18.4 0.1 select_reduce_fusion.3
  18.6 0.1 select_reduce_fusion.2
  18.7 0.1 fusion.19
  18.8 0.9 reshape.70
  19.7 0.1 copy.113
  19.9 2.3 %copy.127 = bf16[128,4096]{0,1:T(8,128)(2,1)} copy(bf16[128,4096]{1,0:T(8,128)(2,1)} %param.12) | data formatting | bytes 2097152 | tf_op jit(solution)/shard_map/reshape | solution.py:16
  22.2 1.6 copy.128
  23.8 3.4 %fusion.31 = (f32[4,8,128]{2,1,0:T(8,128)S(1)}, f32[4,8,128,128]{2,3,1,0:T(8,128)}) fusion(pred[128,128]{0,1:T(8,128)(4,1)S(1)} %fusion.19, bf16[128,4,128,1]{0,2,3,1:T(8,128)(2,1)S(1)} %copy.113, bf16[128,4,8,128]{0,3,2,1:T(8,128)(2,1)} %bitcast.113), kind=kOutput, calls=%fused_computation.59 | convolution fusion | flops 136315008 | bytes 3309568 | tf_op jit(solution)/shard_map/sub | solution.py:30
  27.2 0.0 copy-start.3
  27.2 2.7 %fusion.10 = bf16[4,128,128]{1,2,0:T(8,128)(2,1)} fusion(bf16[128,4,8,128]{0,3,2,1:T(8,128)(2,1)S(1)} %bitcast.108, f32[4,8,128,128]{2,3,1,0:T(8,128)} %get-tuple-element.38, f32[4,8,128]{2,1,0:T(8,128)S(1)} %get-tuple-element.37), kind=kOutput, calls=%fused_computation.21 | convolution fusion | flops 135331840 | bytes 3293184 | tf_op jit(solution)/shard_map/lbjm,jlbw->mlw/dot_general | solution.py:42
  29.9 0.0 copy-done.3
  29.9 0.0 all-gather.7.cloned.1.call-update
  30.0 4.1 %copy.90 = bf16[128,8192]{0,1:T(8,128)(2,1)} copy(bf16[128,8192]{1,0:T(8,128)(2,1)} %param.8) | data formatting | bytes 4194304 | tf_op args[0]
  34.0 4.4 %all-to-all-start = ((bf16[128,8,1024]{0,2,1:T(8,128)(2,1)}), bf16[128,8,1024]{0,2,1:T(8,128)(2,1)}, u32[]{:S(2)}, u32[]{:S(2)}) async-start(bf16[128,8,1024]{0,2,1:T(8,128)(2,1)} %bitcast.107), calls=%async_computation | async-start | bytes 4194304 | tf_op jit(solution)/shard_map/all_to_all | solution.py:93
  38.4 0.0 all-gather.5.cloned.1.call-start
  38.5 0.0 copy-done
  38.5 0.7 collective-permute-start
  39.2 0.0 collective-permute-done
  39.2 0.0 copy-start.2
  39.2 0.7 copy-done.2
  39.9 0.0 all-gather.5.cloned.1.call-update
  39.9 0.0 reduce-scatter.2.cloned.1.call-start
  40.0 0.2 select_reduce_fusion.1
  40.2 0.1 select_reduce_fusion
  40.3 30.3 %all-to-all-done = bf16[128,8,1024]{0,2,1:T(8,128)(2,1)} async-done(((bf16[128,8,1024]{0,2,1:T(8,128)(2,1)}), bf16[128,8,1024]{0,2,1:T(8,128)(2,1)}, u32[]{:S(2)}, u32[]{:S(2)}) %all-to-all-start) | async-done | bytes 2097184 | tf_op jit(solution)/shard_map/all_to_all | solution.py:93
  70.7 3.9 %copy.91 = bf16[8,128,1024]{2,1,0:T(8,128)(2,1)} copy(bf16[8,128,1024]{1,2,0:T(8,128)(2,1)} %bitcast.7) | data formatting | bytes 4194304 | tf_op jit(solution)/shard_map/all_to_all | solution.py:93
  74.6 5.3 %fusion.7 = bf16[1024,1024]{1,0:T(8,128)(2,1)} fusion(bf16[1024,1024]{1,0:T(8,128)(2,1)} %bitcast.112, s32[1024]{0:T(1024)S(1)} %bitcast.130), kind=kOutput, calls=%fused_computation.12 | convolution fusion | flops 2149580800 | bytes 4198400 | tf_op jit(solution)/shard_map/dot_general | solution.py:101
  79.8 0.0 all-gather.7.cloned.1.call-done
  79.8 4.5 %fusion.33 = f32[1024,512]{1,0:T(8,128)} fusion(bf16[1024,1024]{1,0:T(8,128)(2,1)} %fusion.7, bf16[1024,512]{0,1:T(8,128)(2,1)} %all-gather.7.cloned.1.call-done), kind=kOutput, calls=%fused_computation.61 | convolution fusion | flops 1073741824 | bytes 5242880 | tf_op jit(solution)/shard_map/dot_general | solution.py:116
  84.4 0.0 reduce-scatter.2.cloned.1.call-update
  84.4 16.3 %all-gather.5.cloned.1.call-done = bf16[1024,512]{1,0:T(8,128)(2,1)} async-done(((bf16[256,512]{1,0:T(8,128)(2,1)}), bf16[1024,512]{1,0:T(8,128)(2,1)}) %all-gather.5.cloned.1.call-update) | async-done | bytes 1048592 | tf_op jit(solution)/shard_map/all_gather | solution.py:98
  100.7 4.1 %convolution_convert_fusion.3 = bf16[1024,512]{1,0:T(8,128)(2,1)} fusion(bf16[1024,1024]{1,0:T(8,128)(2,1)} %fusion.7, bf16[1024,512]{1,0:T(8,128)(2,1)} %all-gather.5.cloned.1.call-done), kind=kOutput, calls=%fused_computation.17 | convolution fusion | flops 1074266112 | bytes 4194304 | tf_op jit(solution)/shard_map/dot_general | solution.py:102
  104.7 4.2 %all-to-all-start.1 = ((bf16[8,128,512]{2,1,0:T(8,128)(2,1)}), bf16[8,128,512]{2,1,0:T(8,128)(2,1)}, u32[]{:S(2)}, u32[]{:S(2)}) async-start(bf16[8,128,512]{2,1,0:T(8,128)(2,1)} %bitcast.115), calls=%async_computation.1 | async-start | bytes 2097152 | tf_op jit(solution)/shard_map/all_to_all | solution.py:103
  109.0 4.2 %convolution_convert_fusion = bf16[1024,1024]{1,0:T(8,128)(2,1)} fusion(bf16[1024,512]{0,1:T(8,128)(2,1)} %all-gather.7.cloned.1.call-done, bf16[1024,512]{1,0:T(8,128)(2,1)} %all-gather.5.cloned.1.call-done), kind=kOutput, calls=%fused_computation.13 | convolution fusion | flops 1074790400 | bytes 4194304 | tf_op jit(solution)/shard_map/dot_general | solution.py:124
  113.2 11.2 %all-to-all-done.1 = bf16[8,128,512]{2,1,0:T(8,128)(2,1)} async-done(((bf16[8,128,512]{2,1,0:T(8,128)(2,1)}), bf16[8,128,512]{2,1,0:T(8,128)(2,1)}, u32[]{:S(2)}, u32[]{:S(2)}) %all-to-all-start.1) | async-done | bytes 1048608 | tf_op jit(solution)/shard_map/all_to_all | solution.py:103
  124.4 0.0 copy-start.4
  124.4 4.7 %all-to-all-start.2 = ((bf16[8,128,1024]{2,1,0:T(8,128)(2,1)}), bf16[8,128,1024]{2,1,0:T(8,128)(2,1)}, u32[]{:S(2)}, u32[]{:S(2)}) async-start(bf16[8,128,1024]{2,1,0:T(8,128)(2,1)} %bitcast.110), calls=%async_computation.2 | async-start | bytes 4194304 | tf_op jit(solution)/shard_map/all_to_all | solution.py:127
  129.1 1.4 reduce_sum.80
  130.5 0.1 copy.92
  130.6 0.0 copy-done.4
  130.6 3.0 %convolution_convert_fusion.2 = bf16[4,128,8,128]{3,1,2,0:T(8,128)(2,1)} fusion(bf16[128,4,128,1]{0,2,3,1:T(8,128)(2,1)S(1)} %bitcast.118, f32[4,8,128,128]{2,3,1,0:T(8,128)} %get-tuple-element.38, f32[4,8,128]{2,1,0:T(8,128)S(1)} %copy-done.4), kind=kOutput, calls=%fused_computation.16 | convolution fusion | flops 135790592 | bytes 3293184 | tf_op jit(solution)/shard_map/yxmd,dya->myxa/dot_general | solution.py:33
  133.6 2.3 %copy.105 = bf16[128,4096]{1,0:T(8,128)(2,1)} copy(bf16[128,4096]{0,1:T(8,128)(2,1)} %bitcast.117) | data formatting | bytes 2097152
  135.9 1.8 %fusion.32 = f32[4,128,128,8]{2,1,3,0:T(8,128)} fusion(bf16[128,4,128,1]{0,2,3,1:T(8,128)(2,1)S(1)} %bitcast.119, bf16[128,4,8,128]{0,3,2,1:T(8,128)(2,1)S(1)} %bitcast.109), kind=kOutput, calls=%fused_computation.60 | convolution fusion | flops 134217728 | bytes 3276800 | tf_op jit(solution)/shard_map/euaz,nuz->uaen/dot_general | solution.py:39
  137.7 5.4 %convolution_convert_fusion.1 = bf16[4,8,128,128]{2,3,1,0:T(8,128)(2,1)} fusion(bf16[128,4,128,1]{0,2,3,1:T(8,128)(2,1)S(1)} %copy.113, f32[4,128,128,8]{2,1,3,0:T(8,128)} %fusion.32, f32[4,8,128,128]{2,3,1,0:T(8,128)} %get-tuple-element.38, f32[4,8,128]{2,1,0:T(8,128)S(1)} %copy-done.4), kind=kOutput, calls=%fused_computation.15 | convolution fusion | flops 138416256 | bytes 5390336 | tf_op jit(solution)/shard_map/yxmd,dya->myxa/dot_general | solution.py:50
  143.1 0.0 copy-start.1
  143.1 2.4 %copy.106 = bf16[128,4096]{1,0:T(8,128)(2,1)} copy(bf16[128,4096]{0,1:T(8,128)(2,1)} %bitcast.116) | data formatting | bytes 2097152
  145.4 0.0 copy-done.1
  145.4 4.4 %fusion.9 = bf16[4,128,128]{1,2,0:T(8,128)(2,1)S(1)} fusion(bf16[128,4,8,128]{0,3,2,1:T(8,128)(2,1)S(1)} %bitcast.114, f32[4,128,128,8]{2,1,3,0:T(8,128)} %fusion.32, f32[4,8,128,128]{2,3,1,0:T(8,128)} %get-tuple-element.38, f32[4,8,128]{2,1,0:T(8,128)S(1)} %copy-done.4), kind=kOutput, calls=%fused_computation.20 | convolution fusion | flops 137957504 | bytes 5390336 | tf_op jit(solution)/shard_map/lbjm,jlbw->mlw/dot_general | solution.py:53
  149.8 0.8 copy.107
  150.6 5.0 %all-to-all-done.2 = bf16[8,128,1024]{2,1,0:T(8,128)(2,1)} async-done(((bf16[8,128,1024]{2,1,0:T(8,128)(2,1)}), bf16[8,128,1024]{2,1,0:T(8,128)(2,1)}, u32[]{:S(2)}, u32[]{:S(2)}) %all-to-all-start.2) | async-done | bytes 2097184 | tf_op jit(solution)/shard_map/all_to_all | solution.py:127
  155.6 3.1 %copy.129 = bf16[8,16,8,1024]{3,2,0,1:T(8,128)(2,1)} copy(bf16[8,16,8,1024]{3,2,1,0:T(8,128)(2,1)} %bitcast.49) | data formatting | bytes 4194304 | tf_op jit(solution)/shard_map/all_to_all | solution.py:127
  158.7 0.0 reduce-scatter.2.cloned.1.call-done
  158.7 1.9 %broadcast_multiply_fusion = f32[256,512]{1,0:T(8,128)} fusion(f32[256,512]{1,0:T(8,128)} %reduce-scatter.2.cloned.1.call-done), kind=kLoop, calls=%fused_computation.29 | loop fusion | flops 131072 | bytes 1048576 | tf_op jit(solution)/shard_map/mul | solution.py:123
  (5 shorter events, 0.1 us)
Async XLA Ops:
  7.2 31.3 %copy-start = (bf16[2048,512]{1,0:T(8,128)(2,1)S(1)}, bf16[2048,512]{1,0:T(8,128)(2,1)}, u32[]{:S(2)}) copy-start(bf16[2048,512]{1,0:T(8,128)(2,1)} %param.14) | copy-start | bytes 6291460
  7.2 72.7 %all-gather.7.cloned.1.call-start = ((), (), s32[]{:S(2)}) async-start(), calls=%async_computation.5 | async-start | bytes 1179648 | tf_op jit(solution)/shard_map/all_gather | solution.py:114
  27.2 2.7 %copy-start.3 = (f32[4,8,128]{2,1,0:T(8,128)}, f32[4,8,128]{2,1,0:T(8,128)S(1)}, u32[]{:S(2)}) copy-start(f32[4,8,128]{2,1,0:T(8,128)S(1)} %get-tuple-element.37) | copy-start | bytes 49156
  34.0 36.6 %all-to-all-start = ((bf16[128,8,1024]{0,2,1:T(8,128)(2,1)}), bf16[128,8,1024]{0,2,1:T(8,128)(2,1)}, u32[]{:S(2)}, u32[]{:S(2)}) async-start(bf16[128,8,1024]{0,2,1:T(8,128)(2,1)} %bitcast.107), calls=%async_computation | async-start | bytes 4194304 | tf_op jit(solution)/shard_map/all_to_all | solution.py:93
  38.4 62.2 %all-gather.5.cloned.1.call-start = ((), (), s32[]{:S(2)}) async-start(), calls=%async_computation.4 | async-start | bytes 1310720 | tf_op jit(solution)/shard_map/all_gather | solution.py:98
  38.5 0.7 collective-permute-start
  39.2 0.7 copy-start.2
  39.9 118.8 %reduce-scatter.2.cloned.1.call-start = ((), (), s32[]{:S(2)}) async-start(), calls=%async_computation.6 | async-start | bytes 2621440 | tf_op jit(solution)/shard_map/reduce_scatter | solution.py:115
  104.7 19.7 %all-to-all-start.1 = ((bf16[8,128,512]{2,1,0:T(8,128)(2,1)}), bf16[8,128,512]{2,1,0:T(8,128)(2,1)}, u32[]{:S(2)}, u32[]{:S(2)}) async-start(bf16[8,128,512]{2,1,0:T(8,128)(2,1)} %bitcast.115), calls=%async_computation.1 | async-start | bytes 2097152 | tf_op jit(solution)/shard_map/all_to_all | solution.py:103
  124.4 6.2 %copy-start.4 = (f32[4,8,128]{2,1,0:T(8,128)S(1)}, f32[4,8,128]{2,1,0:T(8,128)}, u32[]{:S(2)}) copy-start(f32[4,8,128]{2,1,0:T(8,128)} %copy-done.3) | copy-start | bytes 49156
  124.4 31.2 %all-to-all-start.2 = ((bf16[8,128,1024]{2,1,0:T(8,128)(2,1)}), bf16[8,128,1024]{2,1,0:T(8,128)(2,1)}, u32[]{:S(2)}, u32[]{:S(2)}) async-start(bf16[8,128,1024]{2,1,0:T(8,128)(2,1)} %bitcast.110), calls=%async_computation.2 | async-start | bytes 4194304 | tf_op jit(solution)/shard_map/all_to_all | solution.py:127
  143.1 2.4 %copy-start.1 = (bf16[128,4096]{0,1:T(8,128)(2,1)S(1)}, bf16[128,4096]{0,1:T(8,128)(2,1)}, u32[]{:S(2)}) copy-start(bf16[128,4096]{0,1:T(8,128)(2,1)} %copy.127) | copy-start | bytes 3145732
Sparse Core Ops, SparseCore 0:
  30.1 37.2 all-gather.6
  69.5 31.0 all-gather.4
  103.0 43.3 reduce-scatter.1
where the time goes:
time: 168 us; the launch traced here: 167 us
  waiting for transfers between devices  62.9 us (37%)
  matrix products  38.7 us (23%)
  local copies, waits for them, and re-layouts  22.4 us (13%)
  starting transfers between devices  14.1 us (8%)
  between operations  13.9 us (8%)
  blocking collectives  10.3 us (6%)
  other arithmetic  4.77 us (3%)
    all_to_all x1, waiting for transfers between devices, local(): lax.all_to_all(rollout_rows, 'dp', split_axis=1, concat_axis=0, tiled=True)  30.3 us
    all_gather x1, waiting for transfers between devices, local(): weight = lax.all_gather(piece, 'fsdp', axis=0, tiled=True)  16.3 us
    all_to_all x1, waiting for transfers between devices, local(): lax.all_to_all(partial.reshape(n_dp, tok_rows, partial.shape[1]), 'dp', s...  11.2 us
    all_gather x1, blocking collectives, local(): lax.all_gather(jnp.concatenate([lengths, dest, offset], axis=0), 'dp', ax...  10.3 us
    unnamed x14, local copies, waits for them, and re-layouts  10.2 us
    dot_general x1, matrix products, attend(): jnp.einsum('yxmd,dya->myxa', gradient_scores, heads_keys, preferred_eleme...  5.38 us
    dot_general x1, matrix products, local(): jnp.dot(pick, shared, preferred_element_type=jnp.float32)  5.25 us
    all_to_all x1, waiting for transfers between devices, local(): lax.all_to_all(share, 'dp', split_axis=0, concat_axis=1, tiled=True)  5 us
  transfers between devices with their start and end apart: 7, of which 4 were waited for; matrix products, arithmetic and copies ran while one was open for 31% of the time, Pallas kernels for 0%

commit v1 on v0

--- a/solution.py
+++ b/solution.py
@@ -95,7 +95,15 @@
     piece = lax.dynamic_slice_in_dim(value_weight, me * block, block, axis=0)
     pairs = [(a * n_fsdp + b, b * n_dp + a) for a in range(n_dp) for b in range(n_fsdp)]
     piece = lax.ppermute(piece, ("dp", "fsdp"), pairs)
-    weight = lax.all_gather(piece, "fsdp", axis=0, tiled=True)
+    ways, here = (lax.axis_size("fsdp"), lax.axis_index("fsdp"))
+    grown, reach = (piece, 1)
+    while reach < ways:
+        theirs = lax.ppermute(grown, "fsdp", [(d, d ^ reach) for d in range(ways)])
+        mine_first = jnp.concatenate([grown, theirs], axis=0)
+        theirs_first = jnp.concatenate([theirs, grown], axis=0)
+        grown = jnp.where(here & reach == 0, mine_first, theirs_first)
+        reach = 2 * reach
+    weight = grown
     landing = tables(plan, tok_rows)
     pick = (jnp.arange(column, dtype=jnp.int32)[:, None] == landing[None, :]).astype(jnp.bfloat16)
     rows = jnp.dot(pick, shared, preferred_element_type=jnp.float32).astype(jnp.bfloat16)

time: 168 us -> 219 us (1.30)
  waiting for transfers between devices: 62.9 us -> 88 us
  blocking collectives: 10.3 us -> 29.6 us
  starting transfers between devices: 14.1 us -> 20.5 us
  local copies, waits for them, and re-layouts: 22.4 us -> 20 us
    ppermute x0 -> x2, waiting for transfers between devices: none -> 56.9 us  [local(): theirs = lax.ppermute(grown, 'fsdp', [(d, d ^ reach) for d in range(ways)])]
    all_to_all x1, waiting for transfers between devices: 30.3 us -> 0.01 us  [local(): lax.all_to_all(rollout_rows, 'dp', split_axis=1, concat_axis=0, tiled=True)]
    all_gather x1, blocking collectives: 10.3 us -> 29.6 us  [local(): lax.all_gather(jnp.concatenate([lengths, dest, offset], axis=0), 'dp', ax...]
    all_gather x1 -> x0, waiting for transfers between devices: 16.3 us -> none  [local(): weight = lax.all_gather(piece, 'fsdp', axis=0, tiled=True)]
    all_gather x1, waiting for transfers between devices: 0.01 us -> 15 us  [local(): gathered = lax.all_gather(value_gradient, 'dp', axis=0, tiled=True)]
    ppermute x0 -> x2, starting transfers between devices: none -> 4.8 us  [local(): theirs = lax.ppermute(grown, 'fsdp', [(d, d ^ reach) for d in range(ways)])]
    unnamed x14 -> x24, local copies, waits for them, and re-layouts: 10.2 us -> 9.65 us
  transfers between devices with their start and end apart: 7 -> 8, of which waited for: 4 -> 5; matrix products, arithmetic and copies ran while one was open for 31% -> 27% of each run, Pallas kernels for 0% -> 0%
where the time goes in v1:
time: 219 us; the launch traced here: 218 us
  waiting for transfers between devices  88 us (40%)
  matrix products  39.1 us (18%)
  blocking collectives  29.6 us (14%)
  starting transfers between devices  20.5 us (9%)
  local copies, waits for them, and re-layouts  20 us (9%)
  between operations  14.2 us (6%)
  other arithmetic  6.5 us (3%)
    ppermute x2, waiting for transfers between devices, local(): theirs = lax.ppermute(grown, 'fsdp', [(d, d ^ reach) for d in range(ways)])  56.9 us
    all_gather x1, blocking collectives, local(): lax.all_gather(jnp.concatenate([lengths, dest, offset], axis=0), 'dp', ax...  29.6 us
    all_gather x1, waiting for transfers between devices, local(): gathered = lax.all_gather(value_gradient, 'dp', axis=0, tiled=True)  15 us
    all_to_all x1, waiting for transfers between devices, local(): lax.all_to_all(partial.reshape(n_dp, tok_rows, partial.shape[1]), 'dp', s...  10.9 us
    unnamed x24, local copies, waits for them, and re-layouts  9.65 us
    dot_general x1, matrix products, attend(): jnp.einsum('yxmd,dya->myxa', gradient_scores, heads_keys, preferred_eleme...  5.36 us
    all_to_all x1, starting transfers between devices, local(): lax.all_to_all(rollout_rows, 'dp', split_axis=1, concat_axis=0, tiled=True)  5.31 us
    dot_general x1, matrix products, local(): jnp.dot(pick, shared, preferred_element_type=jnp.float32)  5.25 us
  transfers between devices with their start and end apart: 8, of which 5 were waited for; matrix products, arithmetic and copies ran while one was open for 27% of the time, Pallas kernels for 0%

profile of v1, /device:TPU:0, one launch (start us, length us, event | category | flops | bytes accessed | tf_op | source)
XLA Modules:
  0.0 218.0 jit_solution(14829762827828014881)
XLA Ops:
  7.2 0.0 copy-start
  7.2 4.2 %copy.90 = bf16[128,8192]{0,1:T(8,128)(2,1)} copy(bf16[128,8192]{1,0:T(8,128)(2,1)} %param.8) | data formatting | bytes 4194304 | tf_op args[0]
  11.4 0.0 copy-start.5
  11.4 0.0 copy-start.6
  11.4 0.0 copy-start.7
  11.4 0.0 copy-start.3
  11.4 0.0 copy-start.1
  11.4 5.3 %all-to-all-start = ((bf16[128,8,1024]{0,2,1:T(8,128)(2,1)}), bf16[128,8,1024]{0,2,1:T(8,128)(2,1)}, u32[]{:S(2)}, u32[]{:S(2)}) async-start(bf16[128,8,1024]{0,2,1:T(8,128)(2,1)} %bitcast.105), calls=%async_computation | async-start | bytes 4194304 | tf_op jit(solution)/shard_map/all_to_all | solution.py:93
  16.7 0.0 all-gather.4.cloned.1.call-start
  16.8 0.0 copy-done.5
  16.8 0.0 copy-done.6
  16.8 0.0 copy-done.7
  16.8 29.6 %all-gather.1 = s32[8,3,8]{2,1,0:T(4,128)S(1)} all-gather(s32[1,3,8]{2,1,0:T(4,128)S(1)} %add_bitcast_fusion), channel_id=2, replica_groups=mesh['dp'=8,'fsdp'=4] {'dp'}, dimensions={0}, use_global_device_ids=true | all-gather | bytes 864 | tf_op jit(solution)/shard_map/all_gather | solution.py:92
  46.5 0.1 select_reduce_fusion.3
  46.6 0.1 select_reduce_fusion.2
  46.7 0.7 fusion.19
  47.4 0.0 copy-done.3
  47.5 0.0 copy-start.4
  47.5 0.1 copy.113
  47.6 0.0 copy-done.1
  47.6 1.4 copy.127
  49.0 0.0 copy-done.4
  49.0 3.4 %fusion.33 = (f32[4,8,128]{2,1,0:T(8,128)S(1)}, f32[4,8,128,128]{2,3,1,0:T(8,128)}) fusion(pred[128,128]{0,1:T(8,128)(4,1)S(1)} %copy-done.4, bf16[128,4,128,1]{0,2,3,1:T(8,128)(2,1)S(1)} %copy.113, bf16[128,4,8,128]{0,3,2,1:T(8,128)(2,1)} %bitcast.111), kind=kOutput, calls=%fused_computation.63 | convolution fusion | flops 136315008 | bytes 3309568 | tf_op jit(solution)/shard_map/sub | solution.py:30
  52.4 1.6 copy.128
  54.1 2.7 %fusion.10 = bf16[4,128,128]{1,2,0:T(8,128)(2,1)} fusion(bf16[128,4,8,128]{0,3,2,1:T(8,128)(2,1)S(1)} %bitcast.106, f32[4,8,128,128]{2,3,1,0:T(8,128)} %get-tuple-element.38, f32[4,8,128]{2,1,0:T(8,128)S(1)} %get-tuple-element.37), kind=kOutput, calls=%fused_computation.21 | convolution fusion | flops 135331840 | bytes 3293184 | tf_op jit(solution)/shard_map/lbjm,jlbw->mlw/dot_general | solution.py:42
  56.8 0.0 copy-done.8
  56.8 0.0 all-gather.4.cloned.1.call-update
  56.8 0.0 reduce-scatter.2.cloned.1.call-start
  56.8 0.0 copy-done
  56.9 1.4 collective-permute-start
  58.2 0.2 select_reduce_fusion.1
  58.5 0.1 select_reduce_fusion
  58.6 0.0 all-to-all-done
  58.6 3.9 %copy.91 = bf16[8,128,1024]{2,1,0:T(8,128)(2,1)} copy(bf16[8,128,1024]{1,2,0:T(8,128)(2,1)} %bitcast.7) | data formatting | bytes 4194304 | tf_op jit(solution)/shard_map/all_to_all | solution.py:93
  62.5 5.3 %fusion.7 = bf16[1024,1024]{1,0:T(8,128)(2,1)} fusion(bf16[1024,1024]{1,0:T(8,128)(2,1)} %bitcast.110, s32[1024]{0:T(1024)S(1)} %bitcast.128), kind=kOutput, calls=%fused_computation.12 | convolution fusion | flops 2149580800 | bytes 4198400 | tf_op jit(solution)/shard_map/dot_general | solution.py:109
  67.8 15.0 %all-gather.4.cloned.1.call-done = bf16[1024,512]{0,1:T(8,128)(2,1)} async-done(((bf16[128,512]{0,1:T(8,128)(2,1)}), bf16[1024,512]{0,1:T(8,128)(2,1)}) %all-gather.4.cloned.1.call-update) | async-done | bytes 1048592 | tf_op jit(solution)/shard_map/all_gather | solution.py:122
  82.8 4.4 %fusion.35 = f32[1024,512]{1,0:T(8,128)} fusion(bf16[1024,1024]{1,0:T(8,128)(2,1)} %fusion.7, bf16[1024,512]{0,1:T(8,128)(2,1)} %all-gather.4.cloned.1.call-done), kind=kOutput, calls=%fused_computation.65 | convolution fusion | flops 1073741824 | bytes 5242880 | tf_op jit(solution)/shard_map/dot_general | solution.py:124
  87.2 0.0 reduce-scatter.2.cloned.1.call-update
  87.3 0.0 collective-permute-done
  87.3 1.6 collective-permute-start.1
  88.8 8.7 %collective-permute-done.1 = bf16[256,512]{1,0:T(8,128)(2,1)S(1)} collective-permute-done((bf16[256,512]{1,0:T(8,128)(2,1)}, bf16[256,512]{1,0:T(8,128)(2,1)S(1)}, u32[]{:S(2)}, u32[]{:S(2)}) %collective-permute-start.1) | collective-permute-done | bytes 262176 | tf_op jit(solution)/shard_map/ppermute | solution.py:101
  97.5 2.0 maximum_select_fusion.1
  99.4 3.3 %collective-permute-start.2 = (bf16[512,512]{1,0:T(8,128)(2,1)}, bf16[512,512]{1,0:T(8,128)(2,1)}, u32[]{:S(2)}, u32[]{:S(2)}) collective-permute-start(bf16[512,512]{1,0:T(8,128)(2,1)} %maximum_select_fusion.1), channel_id=1, source_target_pairs={{0,2},{1,3},{2,0},{3,1},{4,6},{5,7},{6,4},{7,5},{8,10},{9,11},{10,... | collective-permute-start | bytes 1572872 | tf_op jit(solution)/shard_map/ppermute | solution.py:101
  102.7 48.2 %collective-permute-done.2 = bf16[512,512]{1,0:T(8,128)(2,1)} collective-permute-done((bf16[512,512]{1,0:T(8,128)(2,1)}, bf16[512,512]{1,0:T(8,128)(2,1)}, u32[]{:S(2)}, u32[]{:S(2)}) %collective-permute-start.2) | collective-permute-done | bytes 524320 | tf_op jit(solution)/shard_map/ppermute | solution.py:101
  150.9 4.4 %convolution_convert_fusion.3 = bf16[1024,512]{1,0:T(8,128)(2,1)} fusion(bf16[1024,1024]{1,0:T(8,128)(2,1)} %fusion.7, bf16[512,512]{1,0:T(8,128)(2,1)} %collective-permute-done.2, bf16[512,512]{1,0:T(8,128)(2,1)} %maximum_select_fusion.1, pred[]{:T(512)S(6)} %eq.47), kind=kOutput, calls=%fused_computation.17 | convolution fusion | flops 1078984704 | bytes 4194305 | tf_op jit(solution)/shard_map/dot_general | solution.py:110
  155.3 4.2 %all-to-all-start.1 = ((bf16[8,128,512]{2,1,0:T(8,128)(2,1)}), bf16[8,128,512]{2,1,0:T(8,128)(2,1)}, u32[]{:S(2)}, u32[]{:S(2)}) async-start(bf16[8,128,512]{2,1,0:T(8,128)(2,1)} %bitcast.113), calls=%async_computation.1 | async-start | bytes 2097152 | tf_op jit(solution)/shard_map/all_to_all | solution.py:111
  159.5 4.5 %convolution_convert_fusion = bf16[1024,1024]{1,0:T(8,128)(2,1)} fusion(bf16[1024,512]{0,1:T(8,128)(2,1)} %all-gather.4.cloned.1.call-done, bf16[512,512]{1,0:T(8,128)(2,1)} %collective-permute-done.2, bf16[512,512]{1,0:T(8,128)(2,1)} %maximum_select_fusion.1, pred[]{:T(512)S(6)} %eq.47), kind=kOutput, calls=%fused_computation.13 | convolution fusion | flops 1079508992 | bytes 4194305 | tf_op jit(solution)/shard_map/dot_general | solution.py:132
  164.0 10.9 %all-to-all-done.1 = bf16[8,128,512]{2,1,0:T(8,128)(2,1)} async-done(((bf16[8,128,512]{2,1,0:T(8,128)(2,1)}), bf16[8,128,512]{2,1,0:T(8,128)(2,1)}, u32[]{:S(2)}, u32[]{:S(2)}) %all-to-all-start.1) | async-done | bytes 1048608 | tf_op jit(solution)/shard_map/all_to_all | solution.py:111
  175.0 0.0 copy-start.9
  175.0 4.7 %all-to-all-start.2 = ((bf16[8,128,1024]{2,1,0:T(8,128)(2,1)}), bf16[8,128,1024]{2,1,0:T(8,128)(2,1)}, u32[]{:S(2)}, u32[]{:S(2)}) async-start(bf16[8,128,1024]{2,1,0:T(8,128)(2,1)} %bitcast.108), calls=%async_computation.2 | async-start | bytes 4194304 | tf_op jit(solution)/shard_map/all_to_all | solution.py:135
  179.6 1.4 reduce_sum.80
  181.0 0.1 copy.92
  181.1 0.0 copy-done.9
  181.1 3.0 %convolution_convert_fusion.2 = bf16[4,128,8,128]{3,1,2,0:T(8,128)(2,1)} fusion(bf16[128,4,128,1]{0,2,3,1:T(8,128)(2,1)S(1)} %bitcast.116, f32[4,8,128,128]{2,3,1,0:T(8,128)} %get-tuple-element.38, f32[4,8,128]{2,1,0:T(8,128)S(1)} %copy-done.9), kind=kOutput, calls=%fused_computation.16 | convolution fusion | flops 135790592 | bytes 3293184 | tf_op jit(solution)/shard_map/yxmd,dya->myxa/dot_general | solution.py:33
  184.1 2.3 %copy.105 = bf16[128,4096]{1,0:T(8,128)(2,1)} copy(bf16[128,4096]{0,1:T(8,128)(2,1)} %bitcast.115) | data formatting | bytes 2097152
  186.4 1.8 fusion.34
  188.2 5.4 %convolution_convert_fusion.1 = bf16[4,8,128,128]{2,3,1,0:T(8,128)(2,1)} fusion(bf16[128,4,128,1]{0,2,3,1:T(8,128)(2,1)S(1)} %copy.113, f32[4,128,128,8]{2,1,3,0:T(8,128)} %fusion.34, f32[4,8,128,128]{2,3,1,0:T(8,128)} %get-tuple-element.38, f32[4,8,128]{2,1,0:T(8,128)S(1)} %copy-done.9), kind=kOutput, calls=%fused_computation.15 | convolution fusion | flops 138416256 | bytes 5390336 | tf_op jit(solution)/shard_map/yxmd,dya->myxa/dot_general | solution.py:50
  193.6 2.4 %copy.106 = bf16[128,4096]{1,0:T(8,128)(2,1)} copy(bf16[128,4096]{0,1:T(8,128)(2,1)} %bitcast.114) | data formatting | bytes 2097152
  195.9 0.0 copy-done.2
  195.9 4.3 %fusion.9 = bf16[4,128,128]{1,2,0:T(8,128)(2,1)S(1)} fusion(bf16[128,4,8,128]{0,3,2,1:T(8,128)(2,1)S(1)} %bitcast.112, f32[4,128,128,8]{2,1,3,0:T(8,128)} %fusion.34, f32[4,8,128,128]{2,3,1,0:T(8,128)} %get-tuple-element.38, f32[4,8,128]{2,1,0:T(8,128)S(1)} %copy-done.9), kind=kOutput, calls=%fused_computation.20 | convolution fusion | flops 137957504 | bytes 5390336 | tf_op jit(solution)/shard_map/lbjm,jlbw->mlw/dot_general | solution.py:53
  200.2 0.8 copy.107
  201.0 5.1 %all-to-all-done.2 = bf16[8,128,1024]{2,1,0:T(8,128)(2,1)} async-done(((bf16[8,128,1024]{2,1,0:T(8,128)(2,1)}), bf16[8,128,1024]{2,1,0:T(8,128)(2,1)}, u32[]{:S(2)}, u32[]{:S(2)}) %all-to-all-start.2) | async-done | bytes 2097184 | tf_op jit(solution)/shard_map/all_to_all | solution.py:135
  206.1 3.1 %copy.129 = bf16[8,16,8,1024]{3,2,0,1:T(8,128)(2,1)} copy(bf16[8,16,8,1024]{3,2,1,0:T(8,128)(2,1)} %bitcast.49) | data formatting | bytes 4194304 | tf_op jit(solution)/shard_map/all_to_all | solution.py:135
  209.3 1.9 broadcast_multiply_fusion
  (10 shorter events, 0.1 us)
Async XLA Ops:
  7.2 49.7 %copy-start = (bf16[2048,512]{1,0:T(8,128)(2,1)S(1)}, bf16[2048,512]{1,0:T(8,128)(2,1)}, u32[]{:S(2)}) copy-start(bf16[2048,512]{1,0:T(8,128)(2,1)} %param.14) | copy-start | bytes 6291460
  11.4 5.4 %copy-start.5 = (s32[1,8]{1,0:T(1,128)S(1)}, s32[1,8]{1,0:T(1,128)}, u32[]{:S(2)}) copy-start(s32[1,8]{1,0:T(1,128)} %param.11) | copy-start | bytes 100
  11.4 5.4 %copy-start.6 = (s32[1,8]{1,0:T(1,128)S(1)}, s32[1,8]{1,0:T(1,128)}, u32[]{:S(2)}) copy-start(s32[1,8]{1,0:T(1,128)} %param.10) | copy-start | bytes 100
  11.4 5.4 %copy-start.7 = (s32[1,8]{1,0:T(1,128)S(1)}, s32[1,8]{1,0:T(1,128)}, u32[]{:S(2)}) copy-start(s32[1,8]{1,0:T(1,128)} %param.9) | copy-start | bytes 100
  11.4 36.0 %copy-start.3 = (bf16[128,512]{1,0:T(8,128)(2,1)S(1)}, bf16[128,512]{1,0:T(8,128)(2,1)}, u32[]{:S(2)}) copy-start(bf16[128,512]{1,0:T(8,128)(2,1)} %param.13) | copy-start | bytes 393220
  11.4 36.2 %copy-start.1 = (bf16[128,4096]{1,0:T(8,128)(2,1)S(1)}, bf16[128,4096]{1,0:T(8,128)(2,1)}, u32[]{:S(2)}) copy-start(bf16[128,4096]{1,0:T(8,128)(2,1)} %param.12) | copy-start | bytes 3145732
  11.4 47.2 %all-to-all-start = ((bf16[128,8,1024]{0,2,1:T(8,128)(2,1)}), bf16[128,8,1024]{0,2,1:T(8,128)(2,1)}, u32[]{:S(2)}, u32[]{:S(2)}) async-start(bf16[128,8,1024]{0,2,1:T(8,128)(2,1)} %bitcast.105), calls=%async_computation | async-start | bytes 4194304 | tf_op jit(solution)/shard_map/all_to_all | solution.py:93
  16.7 66.1 %all-gather.4.cloned.1.call-start = ((), (), s32[]{:S(2)}) async-start(), calls=%async_computation.4 | async-start | bytes 1179648 | tf_op jit(solution)/shard_map/all_gather | solution.py:122
  47.5 1.6 copy-start.4
  52.4 4.3 %copy-start.8 = (f32[4,8,128]{2,1,0:T(8,128)}, f32[4,8,128]{2,1,0:T(8,128)S(1)}, u32[]{:S(2)}) copy-start(f32[4,8,128]{2,1,0:T(8,128)S(1)} %get-tuple-element.37) | copy-start | bytes 49156
  56.8 152.5 %reduce-scatter.2.cloned.1.call-start = ((), (), s32[]{:S(2)}) async-start(), calls=%async_computation.5 | async-start | bytes 2621440 | tf_op jit(solution)/shard_map/reduce_scatter | solution.py:123
  56.9 30.4 %collective-permute-start = (bf16[256,512]{1,0:T(8,128)(2,1)S(1)}, bf16[256,512]{1,0:T(8,128)(2,1)}, u32[]{:S(2)}, u32[]{:S(2)}) collective-permute-start(bf16[256,512]{1,0:T(8,128)(2,1)S(1)} %constant_dynamic-slice_fusion), channel_id=1, source_target_pairs={{0,0},{1,8},{2,16},{3,24},{4,1},{5,9},{6,17},{7,25},{8,2},{9,10},{... | collective-permute-start | bytes 786440 | tf_op jit(solution)/shard_map/ppermute | solution.py:97
  87.3 10.2 %collective-permute-start.1 = (bf16[256,512]{1,0:T(8,128)(2,1)}, bf16[256,512]{1,0:T(8,128)(2,1)S(1)}, u32[]{:S(2)}, u32[]{:S(2)}) collective-permute-start(bf16[256,512]{1,0:T(8,128)(2,1)} %collective-permute-done), channel_id=1, source_target_pairs={{0,1},{1,0},{2,3},{3,2},{4,5},{5,4},{6,7},{7,6},{8,9},{9,8},{10,11... | collective-permute-start | bytes 786440 | tf_op jit(solution)/shard_map/ppermute | solution.py:101
  99.4 51.5 %collective-permute-start.2 = (bf16[512,512]{1,0:T(8,128)(2,1)}, bf16[512,512]{1,0:T(8,128)(2,1)}, u32[]{:S(2)}, u32[]{:S(2)}) collective-permute-start(bf16[512,512]{1,0:T(8,128)(2,1)} %maximum_select_fusion.1), channel_id=1, source_target_pairs={{0,2},{1,3},{2,0},{3,1},{4,6},{5,7},{6,4},{7,5},{8,10},{9,11},{10,... | collective-permute-start | bytes 1572872 | tf_op jit(solution)/shard_map/ppermute | solution.py:101
  155.3 19.7 %all-to-all-start.1 = ((bf16[8,128,512]{2,1,0:T(8,128)(2,1)}), bf16[8,128,512]{2,1,0:T(8,128)(2,1)}, u32[]{:S(2)}, u32[]{:S(2)}) async-start(bf16[8,128,512]{2,1,0:T(8,128)(2,1)} %bitcast.113), calls=%async_computation.1 | async-start | bytes 2097152 | tf_op jit(solution)/shard_map/all_to_all | solution.py:111
  175.0 6.2 %copy-start.9 = (f32[4,8,128]{2,1,0:T(8,128)S(1)}, f32[4,8,128]{2,1,0:T(8,128)}, u32[]{:S(2)}) copy-start(f32[4,8,128]{2,1,0:T(8,128)} %copy-done.8) | copy-start | bytes 49156
  175.0 31.1 %all-to-all-start.2 = ((bf16[8,128,1024]{2,1,0:T(8,128)(2,1)}), bf16[8,128,1024]{2,1,0:T(8,128)(2,1)}, u32[]{:S(2)}, u32[]{:S(2)}) async-start(bf16[8,128,1024]{2,1,0:T(8,128)(2,1)} %bitcast.108), calls=%async_computation.2 | async-start | bytes 4194304 | tf_op jit(solution)/shard_map/all_to_all | solution.py:135
  193.6 2.4 %copy-start.2 = (bf16[128,4096]{0,1:T(8,128)(2,1)S(1)}, bf16[128,4096]{0,1:T(8,128)(2,1)}, u32[]{:S(2)}) copy-start(bf16[128,4096]{0,1:T(8,128)(2,1)} %copy.127) | copy-start | bytes 3145732
Sparse Core Ops, SparseCore 0:
  56.9 25.8 all-gather.3
  87.4 61.2 reduce-scatter.1
